TPU v7x, 512 devices: a whole 4x4x16 slice. The times are simulated.
512 devices in a mesh: ctx: 64 (over y, z_lo, core), ch: 8 (over z_hi, x).
Axes of the slice: x: 4, y: 4, z: 16 (z_hi: 2, z_lo: 8; z = z_hi * 8 + z_lo), core: 2. Of those that a mesh axis runs over, the one named last changes fastest.
Arguments:
- x_one: bfloat16 [8192, 4096], P('ctx', 'ch'), may hold values from -6 to 6
- x_two: bfloat16 [8192, 4096], P('ctx', 'ch'), may hold values from -6 to 6
- values: bfloat16 [8192, 4096], P('ctx', 'ch'), may hold values from -6 to 6
- grad_out: bfloat16 [8192, 4096], P('ctx', 'ch'), may hold values from -3 to 3
- filter_raw: bfloat16 [1024, 512], P('ctx', 'ch'), may hold values from -4 to 4
Outputs:
- grad_x_one: bfloat16 [8192, 4096], P('ctx', 'ch')
- grad_x_two: bfloat16 [8192, 4096], P('ctx', 'ch')
- grad_values: bfloat16 [8192, 4096], P('ctx', 'ch')
- grad_filter: float32 [1024, 512], P('ctx', 'ch')
All inputs are finite; a program needn't handle non-finite values.
Results may differ from a plain program's by a relative error of at most 0.0049.
Values may be sent and summed in bfloat16 or wider, within the bound.
A program may use at most 64 MiB of HBM per device.

v0:
```python
import math
import jax
import jax.numpy as jnp
from jax import lax
from jax.sharding import PartitionSpec as P

highest = lax.Precision.HIGHEST


def shifted(value, axis, by):
    peers = lax.axis_size(axis)
    pairs = [(i, i + by) for i in range(peers) if 0 <= i + by < peers]
    return lax.ppermute(value, axis, pairs)


def dft_tables(tok):
    size = 2 * tok
    freq = jnp.arange(tok + 1, dtype=jnp.int32)
    place = jnp.arange(tok, dtype=jnp.int32)

    def angles(rows, cols):
        return 2.0 * math.pi / size * (rows[:, None] * cols[None, :] % size).astype(jnp.float32)

    forward_angle = angles(freq, place)
    forward_table = jnp.concatenate([jnp.cos(forward_angle), -jnp.sin(forward_angle)], axis=0)
    weights = jnp.where((freq == 0) | (freq == tok), 1.0, 2.0).astype(jnp.float32) / size

    def inverse(points):
        angle = angles(points, freq)
        return jnp.concatenate(
            [weights[None, :] * jnp.cos(angle), -weights[None, :] * jnp.sin(angle)], axis=1
        )

    lower_table = inverse(place)
    upper_table = inverse(place + tok)
    lag_table = inverse(tok - place)
    signs = (1 - 2 * (freq % 2)).astype(jnp.float32)
    return (forward_table, lower_table, upper_table, lag_table, signs)


def weigh_plain(fil_real, fil_imag, spec_real, spec_imag):
    real = jnp.sum(fil_real * spec_real - fil_imag * spec_imag, axis=0)
    imag = jnp.sum(fil_real * spec_imag + fil_imag * spec_real, axis=0)
    return (real, imag)


def weigh_conj(fil_real, fil_imag, spec_real, spec_imag):
    real = jnp.sum(fil_real * spec_real + fil_imag * spec_imag, axis=0)
    imag = jnp.sum(fil_real * spec_imag - fil_imag * spec_real, axis=0)
    return (real, imag)


def local(x_one, x_two, values, grad_out, filter_raw):
    tok, chans = x_one.shape
    piece = lax.all_gather(filter_raw, "ctx", axis=0, tiled=True)
    whole = lax.all_gather(piece, "ch", axis=1, tiled=True)
    taps, groups = whole.shape
    span = taps // tok
    repeat = chans // groups
    bins = tok + 1
    scale = 1.0 / math.sqrt(taps)
    forward_table, lower_table, upper_table, lag_table, signs = dft_tables(tok)
    filt = whole.astype(jnp.float32) * scale
    filt_spec = jnp.einsum(
        "mt,ktf->kmf", forward_table, filt.reshape(span, tok, groups), precision=highest
    )
    filt_real = filt_spec[:, :bins, :][:, :, None, :]
    filt_imag = filt_spec[:, bins:, :][:, :, None, :]
    product_in = (x_one.astype(jnp.float32) * values.astype(jnp.float32)).astype(jnp.bfloat16)
    grad_conv = (grad_out.astype(jnp.float32) * x_two.astype(jnp.float32)).astype(jnp.bfloat16)
    lower_list = [product_in]
    upper_list = [grad_conv]
    lower_block = product_in
    upper_block = grad_conv
    for offset in range(1, span + 1):
        lower_block = shifted(lower_block, "ctx", 1)
        upper_block = shifted(upper_block, "ctx", -1)
        lower_list.append(lower_block)
        upper_list.append(upper_block)

    def spectra(blocks):
        stacked = jnp.stack(blocks).astype(jnp.float32)
        spec = jnp.einsum("mt,ktc->kmc", forward_table, stacked, precision=highest)
        return (
            spec[:, :bins].reshape(span + 1, bins, repeat, groups),
            spec[:, bins:].reshape(span + 1, bins, repeat, groups),
        )

    in_real, in_imag = spectra(lower_list)
    grad_real, grad_imag = spectra(upper_list)
    forward_lo = weigh_plain(filt_real, filt_imag, in_real[:span], in_imag[:span])
    forward_hi = weigh_plain(filt_real, filt_imag, in_real[1:], in_imag[1:])
    backward_lo = weigh_conj(filt_real, filt_imag, grad_real[:span], grad_imag[:span])
    backward_hi = weigh_conj(filt_real, filt_imag, grad_real[1:], grad_imag[1:])
    own_real = grad_real[0]
    own_imag = grad_imag[0]
    cross_real = jnp.sum(own_real * in_real + own_imag * in_imag, axis=2)
    cross_imag = jnp.sum(own_real * in_imag - own_imag * in_real, axis=2)

    def inverse_apply(table, parts):
        stacked = jnp.concatenate([parts[0], parts[1]], axis=0).reshape(2 * bins, chans)
        return jnp.dot(table, stacked, precision=highest)

    conv_out = inverse_apply(lower_table, forward_lo) + inverse_apply(upper_table, forward_hi)
    grad_in = inverse_apply(lower_table, backward_lo) + inverse_apply(upper_table, backward_hi)
    grad_x_one = (grad_in * values.astype(jnp.float32)).astype(jnp.bfloat16)
    grad_x_two = (grad_out.astype(jnp.float32) * conv_out).astype(jnp.bfloat16)
    grad_values = (grad_in * x_one.astype(jnp.float32)).astype(jnp.bfloat16)
    lag_real = cross_real[1:] + signs[None, :, None] * cross_real[:-1]
    lag_imag = cross_imag[1:] + signs[None, :, None] * cross_imag[:-1]
    lag_spec = jnp.concatenate([lag_real, lag_imag], axis=1)
    filter_terms = (
        jnp.einsum("rm,kmf->krf", lag_table, lag_spec, precision=highest).reshape(taps, groups)
        * scale
    )
    by_taps = lax.psum_scatter(filter_terms, "ctx", scatter_dimension=0, tiled=True)
    grad_filter = lax.psum_scatter(by_taps, "ch", scatter_dimension=1, tiled=True)
    return (grad_x_one, grad_x_two, grad_values, grad_filter)


def solution(mesh):
    placed = (P("ctx", "ch"), P("ctx", "ch"), P("ctx", "ch"), P("ctx", "ch"), P("ctx", "ch"))
    return jax.shard_map(
        local,
        mesh=mesh,
        in_specs=placed,
        out_specs=(P("ctx", "ch"), P("ctx", "ch"), P("ctx", "ch"), P("ctx", "ch")),
        check_vma=False,
    )
```

profile of v0, /device:TPU:8, one launch (start us, length us, event | category | flops | bytes accessed | tf_op | source)
XLA Modules:
  0.0 816.9 jit_solution(427479515096620973)
XLA Ops:
  9.0 1.9 collective-permute-start.8
  11.0 114.9 %all_gather.6 = bf16[1024,64]{1,0:T(8,128)(2,1)S(1)} all-gather(bf16[16,64]{1,0:T(8,128)(2,1)} %param.9), channel_id=1, replica_groups=mesh['ctx'=64,'ch'=8] {'ctx'}, dimensions={0}, use_global_device_ids=true | all-gather | bytes 133120 | tf_op jit(solution)/shard_map/all_gather | solution.py:55
  127.7 1.9 collective-permute-start
  129.7 1.5 sine_multiply_fusion
  131.5 2.4 collective-permute-start.9
  133.9 10.7 %collective-permute-start.1 = (bf16[128,512]{1,0:T(8,128)(2,1)S(1)}, bf16[128,512]{1,0:T(8,128)(2,1)S(1)}, u32[]{:S(2)}, u32[]{:S(2)}) collective-permute-start(bf16[128,512]{1,0:T(8,128)(2,1)S(1)} %collective-permute-done), channel_id=1, source_target_pairs={{8,0},{16,8},{24,16},{32,24},{40,32},{48,40},{56,48},{64,56},{72,6... | collective-permute-start | bytes 393224 | tf_op jit(solution)/shard_map/ppermute | solution.py:13
  145.4 1.9 collective-permute-start.10
  147.3 11.3 %collective-permute-start.2 = (bf16[128,512]{1,0:T(8,128)(2,1)S(1)}, bf16[128,512]{1,0:T(8,128)(2,1)S(1)}, u32[]{:S(2)}, u32[]{:S(2)}) collective-permute-start(bf16[128,512]{1,0:T(8,128)(2,1)S(1)} %collective-permute-done.1), channel_id=1, source_target_pairs={{8,0},{16,8},{24,16},{32,24},{40,32},{48,40},{56,48},{64,56},{72,6... | collective-permute-start | bytes 393224 | tf_op jit(solution)/shard_map/ppermute | solution.py:13
  159.4 1.9 collective-permute-start.11
  162.4 11.3 %collective-permute-start.3 = (bf16[128,512]{1,0:T(8,128)(2,1)S(1)}, bf16[128,512]{1,0:T(8,128)(2,1)S(1)}, u32[]{:S(2)}, u32[]{:S(2)}) collective-permute-start(bf16[128,512]{1,0:T(8,128)(2,1)S(1)} %collective-permute-done.2), channel_id=1, source_target_pairs={{8,0},{16,8},{24,16},{32,24},{40,32},{48,40},{56,48},{64,56},{72,6... | collective-permute-start | bytes 393224 | tf_op jit(solution)/shard_map/ppermute | solution.py:13
  173.8 1.9 collective-permute-start.12
  176.2 11.4 %collective-permute-start.4 = (bf16[128,512]{1,0:T(8,128)(2,1)S(1)}, bf16[128,512]{1,0:T(8,128)(2,1)S(1)}, u32[]{:S(2)}, u32[]{:S(2)}) collective-permute-start(bf16[128,512]{1,0:T(8,128)(2,1)S(1)} %collective-permute-done.3), channel_id=1, source_target_pairs={{8,0},{16,8},{24,16},{32,24},{40,32},{48,40},{56,48},{64,56},{72,6... | collective-permute-start | bytes 393224 | tf_op jit(solution)/shard_map/ppermute | solution.py:13
  187.8 1.9 collective-permute-start.13
  189.7 8.4 %collective-permute-done.4 = bf16[128,512]{1,0:T(8,128)(2,1)S(1)} collective-permute-done((bf16[128,512]{1,0:T(8,128)(2,1)S(1)}, bf16[128,512]{1,0:T(8,128)(2,1)S(1)}, u32[]{:S(2)}, u32[]{:S(2)}) %collective-permute-start.4) | collective-permute-done | bytes 131104 | tf_op jit(solution)/shard_map/ppermute | solution.py:13
  198.1 11.7 %collective-permute-start.5 = (bf16[128,512]{1,0:T(8,128)(2,1)S(1)}, bf16[128,512]{1,0:T(8,128)(2,1)S(1)}, u32[]{:S(2)}, u32[]{:S(2)}) collective-permute-start(bf16[128,512]{1,0:T(8,128)(2,1)S(1)} %collective-permute-done.4), channel_id=1, source_target_pairs={{8,0},{16,8},{24,16},{32,24},{40,32},{48,40},{56,48},{64,56},{72,6... | collective-permute-start | bytes 393224 | tf_op jit(solution)/shard_map/ppermute | solution.py:13
  209.8 4.0 collective-permute-done.13
  213.8 1.9 collective-permute-start.14
  215.7 11.1 %collective-permute-start.6 = (bf16[128,512]{1,0:T(8,128)(2,1)S(1)}, bf16[128,512]{1,0:T(8,128)(2,1)S(1)}, u32[]{:S(2)}, u32[]{:S(2)}) collective-permute-start(bf16[128,512]{1,0:T(8,128)(2,1)S(1)} %collective-permute-done.5), channel_id=1, source_target_pairs={{8,0},{16,8},{24,16},{32,24},{40,32},{48,40},{56,48},{64,56},{72,6... | collective-permute-start | bytes 393224 | tf_op jit(solution)/shard_map/ppermute | solution.py:13
  227.6 1.9 collective-permute-start.15
  229.5 11.3 %collective-permute-start.7 = (bf16[128,512]{1,0:T(8,128)(2,1)S(1)}, bf16[128,512]{1,0:T(8,128)(2,1)S(1)}, u32[]{:S(2)}, u32[]{:S(2)}) collective-permute-start(bf16[128,512]{1,0:T(8,128)(2,1)S(1)} %collective-permute-done.6), channel_id=1, source_target_pairs={{8,0},{16,8},{24,16},{32,24},{40,32},{48,40},{56,48},{64,56},{72,6... | collective-permute-start | bytes 393224 | tf_op jit(solution)/shard_map/ppermute | solution.py:13
  240.9 2.3 collective-permute-done.7
  243.2 2.3 convolution_bitcast_fusion.1
  245.6 2.4 convolution_bitcast_fusion
  251.0 7.3 fusion.6
  258.6 2.9 convert_multiply_fusion
  261.5 1.9 copy.12
  263.5 4.1 convolution_bitcast_fusion.2
  267.6 8.1 subtract_reduce_fusion
  278.5 388.4 %reduce-scatter.5.cloned.1.call-done = f32[16,512]{1,0:T(8,128)} async-done(((f32[1024,512]{1,0:T(8,128)}), f32[16,512]{1,0:T(8,128)}) %reduce-scatter.5.cloned.1.call-update) | async-done | bytes 32784 | tf_op jit(solution)/shard_map/reduce_scatter | solution.py:116
  666.9 1.6 copy.13
  669.8 138.2 %reduce-scatter.7.cloned.1.call-done = f32[64,16]{1,0:T(8,128)} async-done(((f32[512,16]{1,0:T(8,128)}), f32[64,16]{1,0:T(8,128)}) %reduce-scatter.7.cloned.1.call-update) | async-done | bytes 4112
  808.0 1.4 copy.14
  (64 shorter events, 14.7 us)
Async XLA Ops:
  8.0 250.6 %all-gather.2.cloned.1.call-start = ((), (), s32[]{:S(2)}) async-start(), calls=%async_computation.2 | async-start | bytes 1179648 | tf_op jit(solution)/shard_map/all_gather | solution.py:56
  9.0 122.4 %collective-permute-start.8 = (bf16[128,512]{1,0:T(8,128)(2,1)S(1)}, bf16[128,512]{1,0:T(8,128)(2,1)S(1)}, u32[]{:S(2)}, u32[]{:S(2)}) collective-permute-start(bf16[128,512]{1,0:T(8,128)(2,1)S(1)} %get-tuple-element.13), channel_id=1, source_target_pairs={{0,8},{8,16},{16,24},{24,32},{32,40},{40,48},{48,56},{56,64},{64,7... | collective-permute-start | bytes 393224 | tf_op jit(solution)/shard_map/ppermute | solution.py:13
  126.7 540.2 %reduce-scatter.5.cloned.1.call-start = ((), (), s32[]{:S(2)}) async-start(), calls=%async_computation.3 | async-start | bytes 2129920 | tf_op jit(solution)/shard_map/reduce_scatter | solution.py:116
  127.7 6.2 collective-permute-start
  131.5 13.9 %collective-permute-start.9 = (bf16[128,512]{1,0:T(8,128)(2,1)S(1)}, bf16[128,512]{1,0:T(8,128)(2,1)S(1)}, u32[]{:S(2)}, u32[]{:S(2)}) collective-permute-start(bf16[128,512]{1,0:T(8,128)(2,1)S(1)} %collective-permute-done.8), channel_id=1, source_target_pairs={{0,8},{8,16},{16,24},{24,32},{32,40},{40,48},{48,56},{56,64},{64,7... | collective-permute-start | bytes 393224 | tf_op jit(solution)/shard_map/ppermute | solution.py:13
  133.9 13.4 %collective-permute-start.1 = (bf16[128,512]{1,0:T(8,128)(2,1)S(1)}, bf16[128,512]{1,0:T(8,128)(2,1)S(1)}, u32[]{:S(2)}, u32[]{:S(2)}) collective-permute-start(bf16[128,512]{1,0:T(8,128)(2,1)S(1)} %collective-permute-done), channel_id=1, source_target_pairs={{8,0},{16,8},{24,16},{32,24},{40,32},{48,40},{56,48},{64,56},{72,6... | collective-permute-start | bytes 393224 | tf_op jit(solution)/shard_map/ppermute | solution.py:13
  145.4 14.1 %collective-permute-start.10 = (bf16[128,512]{1,0:T(8,128)(2,1)S(1)}, bf16[128,512]{1,0:T(8,128)(2,1)S(1)}, u32[]{:S(2)}, u32[]{:S(2)}) collective-permute-start(bf16[128,512]{1,0:T(8,128)(2,1)S(1)} %collective-permute-done.9), channel_id=1, source_target_pairs={{0,8},{8,16},{16,24},{24,32},{32,40},{40,48},{48,56},{56,64},{64,7... | collective-permute-start | bytes 393224 | tf_op jit(solution)/shard_map/ppermute | solution.py:13
  147.3 15.1 %collective-permute-start.2 = (bf16[128,512]{1,0:T(8,128)(2,1)S(1)}, bf16[128,512]{1,0:T(8,128)(2,1)S(1)}, u32[]{:S(2)}, u32[]{:S(2)}) collective-permute-start(bf16[128,512]{1,0:T(8,128)(2,1)S(1)} %collective-permute-done.1), channel_id=1, source_target_pairs={{8,0},{16,8},{24,16},{32,24},{40,32},{48,40},{56,48},{64,56},{72,6... | collective-permute-start | bytes 393224 | tf_op jit(solution)/shard_map/ppermute | solution.py:13
  159.4 14.3 %collective-permute-start.11 = (bf16[128,512]{1,0:T(8,128)(2,1)S(1)}, bf16[128,512]{1,0:T(8,128)(2,1)S(1)}, u32[]{:S(2)}, u32[]{:S(2)}) collective-permute-start(bf16[128,512]{1,0:T(8,128)(2,1)S(1)} %collective-permute-done.10), channel_id=1, source_target_pairs={{0,8},{8,16},{16,24},{24,32},{32,40},{40,48},{48,56},{56,64},{64,7... | collective-permute-start | bytes 393224 | tf_op jit(solution)/shard_map/ppermute | solution.py:13
  162.4 13.8 %collective-permute-start.3 = (bf16[128,512]{1,0:T(8,128)(2,1)S(1)}, bf16[128,512]{1,0:T(8,128)(2,1)S(1)}, u32[]{:S(2)}, u32[]{:S(2)}) collective-permute-start(bf16[128,512]{1,0:T(8,128)(2,1)S(1)} %collective-permute-done.2), channel_id=1, source_target_pairs={{8,0},{16,8},{24,16},{32,24},{40,32},{48,40},{56,48},{64,56},{72,6... | collective-permute-start | bytes 393224 | tf_op jit(solution)/shard_map/ppermute | solution.py:13
  173.8 14.0 %collective-permute-start.12 = (bf16[128,512]{1,0:T(8,128)(2,1)S(1)}, bf16[128,512]{1,0:T(8,128)(2,1)S(1)}, u32[]{:S(2)}, u32[]{:S(2)}) collective-permute-start(bf16[128,512]{1,0:T(8,128)(2,1)S(1)} %collective-permute-done.11), channel_id=1, source_target_pairs={{0,8},{8,16},{16,24},{24,32},{32,40},{40,48},{48,56},{56,64},{64,7... | collective-permute-start | bytes 393224 | tf_op jit(solution)/shard_map/ppermute | solution.py:13
  176.2 21.9 %collective-permute-start.4 = (bf16[128,512]{1,0:T(8,128)(2,1)S(1)}, bf16[128,512]{1,0:T(8,128)(2,1)S(1)}, u32[]{:S(2)}, u32[]{:S(2)}) collective-permute-start(bf16[128,512]{1,0:T(8,128)(2,1)S(1)} %collective-permute-done.3), channel_id=1, source_target_pairs={{8,0},{16,8},{24,16},{32,24},{40,32},{48,40},{56,48},{64,56},{72,6... | collective-permute-start | bytes 393224 | tf_op jit(solution)/shard_map/ppermute | solution.py:13
  187.8 26.0 %collective-permute-start.13 = (bf16[128,512]{1,0:T(8,128)(2,1)S(1)}, bf16[128,512]{1,0:T(8,128)(2,1)S(1)}, u32[]{:S(2)}, u32[]{:S(2)}) collective-permute-start(bf16[128,512]{1,0:T(8,128)(2,1)S(1)} %collective-permute-done.12), channel_id=1, source_target_pairs={{0,8},{8,16},{16,24},{24,32},{32,40},{40,48},{48,56},{56,64},{64,7... | collective-permute-start | bytes 393224 | tf_op jit(solution)/shard_map/ppermute | solution.py:13
  198.1 17.6 %collective-permute-start.5 = (bf16[128,512]{1,0:T(8,128)(2,1)S(1)}, bf16[128,512]{1,0:T(8,128)(2,1)S(1)}, u32[]{:S(2)}, u32[]{:S(2)}) collective-permute-start(bf16[128,512]{1,0:T(8,128)(2,1)S(1)} %collective-permute-done.4), channel_id=1, source_target_pairs={{8,0},{16,8},{24,16},{32,24},{40,32},{48,40},{56,48},{64,56},{72,6... | collective-permute-start | bytes 393224 | tf_op jit(solution)/shard_map/ppermute | solution.py:13
  213.8 13.8 %collective-permute-start.14 = (bf16[128,512]{1,0:T(8,128)(2,1)S(1)}, bf16[128,512]{1,0:T(8,128)(2,1)S(1)}, u32[]{:S(2)}, u32[]{:S(2)}) collective-permute-start(bf16[128,512]{1,0:T(8,128)(2,1)S(1)} %collective-permute-done.13), channel_id=1, source_target_pairs={{0,8},{8,16},{16,24},{24,32},{32,40},{40,48},{48,56},{56,64},{64,7... | collective-permute-start | bytes 393224 | tf_op jit(solution)/shard_map/ppermute | solution.py:13
  215.7 13.8 %collective-permute-start.6 = (bf16[128,512]{1,0:T(8,128)(2,1)S(1)}, bf16[128,512]{1,0:T(8,128)(2,1)S(1)}, u32[]{:S(2)}, u32[]{:S(2)}) collective-permute-start(bf16[128,512]{1,0:T(8,128)(2,1)S(1)} %collective-permute-done.5), channel_id=1, source_target_pairs={{8,0},{16,8},{24,16},{32,24},{40,32},{48,40},{56,48},{64,56},{72,6... | collective-permute-start | bytes 393224 | tf_op jit(solution)/shard_map/ppermute | solution.py:13
  227.6 18.0 %collective-permute-start.15 = (bf16[128,512]{1,0:T(8,128)(2,1)S(1)}, bf16[128,512]{1,0:T(8,128)(2,1)S(1)}, u32[]{:S(2)}, u32[]{:S(2)}) collective-permute-start(bf16[128,512]{1,0:T(8,128)(2,1)S(1)} %collective-permute-done.14), channel_id=1, source_target_pairs={{0,8},{8,16},{16,24},{24,32},{32,40},{40,48},{48,56},{56,64},{64,7... | collective-permute-start | bytes 393224 | tf_op jit(solution)/shard_map/ppermute | solution.py:13
  229.5 13.7 %collective-permute-start.7 = (bf16[128,512]{1,0:T(8,128)(2,1)S(1)}, bf16[128,512]{1,0:T(8,128)(2,1)S(1)}, u32[]{:S(2)}, u32[]{:S(2)}) collective-permute-start(bf16[128,512]{1,0:T(8,128)(2,1)S(1)} %collective-permute-done.6), channel_id=1, source_target_pairs={{8,0},{16,8},{24,16},{32,24},{40,32},{48,40},{56,48},{64,56},{72,6... | collective-permute-start | bytes 393224 | tf_op jit(solution)/shard_map/ppermute | solution.py:13
  245.5 2.5 copy-start.1
  248.0 2.2 copy-start
  258.3 549.7 %reduce-scatter.7.cloned.1.call-start = ((), (), s32[]{:S(2)}) async-start(), calls=%async_computation.4 | async-start | bytes 294912
  267.6 8.1 copy-start.2
  267.6 8.1 copy-start.3
  267.6 9.5 %copy-start.4 = (bf16[128,512]{1,0:T(8,128)(2,1)S(1)}, bf16[128,512]{1,0:T(8,128)(2,1)}, u32[]{:S(2)}) copy-start(bf16[128,512]{1,0:T(8,128)(2,1)} %param.5) | copy-start | bytes 393220
  267.6 9.5 %copy-start.5 = (bf16[128,512]{1,0:T(8,128)(2,1)S(1)}, bf16[128,512]{1,0:T(8,128)(2,1)}, u32[]{:S(2)}) copy-start(bf16[128,512]{1,0:T(8,128)(2,1)} %param.7) | copy-start | bytes 393220
  275.7 392.7 %copy-start.6 = (bf16[128,512]{1,0:T(8,128)(2,1)S(1)}, bf16[128,512]{1,0:T(8,128)(2,1)}, u32[]{:S(2)}) copy-start(bf16[128,512]{1,0:T(8,128)(2,1)} %param.8) | copy-start | bytes 393220
Sparse Core Ops, SparseCore 0:
  126.8 90.6 all-gather.1
  668.6 139.3 reduce-scatter.6
Sparse Core Ops, SparseCore 1:
  258.4 408.4 reduce-scatter.4
where the time goes:
time: 818 us; the launch traced here: 817 us
  waiting for transfers between devices  545 us (67%)
  blocking collectives  115 us (14%)
  starting transfers between devices  96.9 us (12%)
  matrix products  20.1 us (2%)
  other arithmetic  16.4 us (2%)
  between operations  16 us (2%)
    reduce_scatter x1, waiting for transfers between devices, local(): lax.psum_scatter(filter_terms, 'ctx', scatter_dimension=0, tiled=True)  388 us
    unnamed x4, waiting for transfers between devices  138 us
    all_gather x1, blocking collectives, local(): piece = lax.all_gather(filter_raw, 'ctx', axis=0, tiled=True)  115 us
    ppermute x16, starting transfers between devices, shifted(): return lax.ppermute(value, axis, pairs)  96.6 us
    ppermute x16, waiting for transfers between devices, shifted(): return lax.ppermute(value, axis, pairs)  18.5 us
  transfers between devices with their start and end apart: 19, of which 11 were waited for; matrix products, arithmetic and copies ran while one was open for 5% of the time, Pallas kernels for 0%

commit v1 on v0

--- a/solution.py
+++ b/solution.py
@@ -53,7 +53,9 @@
 def local(x_one, x_two, values, grad_out, filter_raw):
     tok, chans = x_one.shape
     piece = lax.all_gather(filter_raw, "ctx", axis=0, tiled=True)
-    whole = lax.all_gather(piece, "ch", axis=1, tiled=True)
+    whole = jnp.concatenate(
+        lax.all_to_all(jnp.stack([piece] * lax.axis_size("ch")), "ch", 0, 0), axis=1
+    )
     taps, groups = whole.shape
     span = taps // tok
     repeat = chans // groups

time: 818 us -> 849 us (1.038)
  waiting for transfers between devices: 545 us -> 576 us
  starting transfers between devices: 96.9 us -> 108 us
  other arithmetic: 16.4 us -> 7.88 us
    ppermute x16, waiting for transfers between devices: 18.5 us -> 41.3 us  [shifted(): return lax.ppermute(value, axis, pairs)]
    all_to_all x0 -> x1, starting transfers between devices: none -> 10 us  [local(): lax.all_to_all(jnp.stack([piece] * lax.axis_size('ch')), 'ch', 0, 0)]
    unnamed x4 -> x3, waiting for transfers between devices: 138 us -> 142 us
  transfers between devices with their start and end apart: 19 -> 19, of which waited for: 11 -> 11; matrix products, arithmetic and copies ran while one was open for 5% -> 3% of each run, Pallas kernels for 0% -> 0%
where the time goes in v1:
time: 849 us; the launch traced here: 848 us
  waiting for transfers between devices  576 us (68%)
  blocking collectives  115 us (14%)
  starting transfers between devices  108 us (13%)
  matrix products  19.8 us (2%)
  between operations  14.7 us (2%)
    reduce_scatter x1, waiting for transfers between devices, local(): lax.psum_scatter(filter_terms, 'ctx', scatter_dimension=0, tiled=True)  393 us
    unnamed x3, waiting for transfers between devices  142 us
    all_gather x1, blocking collectives, local(): piece = lax.all_gather(filter_raw, 'ctx', axis=0, tiled=True)  115 us
    ppermute x16, starting transfers between devices, shifted(): return lax.ppermute(value, axis, pairs)  97.7 us
    ppermute x16, waiting for transfers between devices, shifted(): return lax.ppermute(value, axis, pairs)  41.3 us
  transfers between devices with their start and end apart: 19, of which 11 were waited for; matrix products, arithmetic and copies ran while one was open for 3% of the time, Pallas kernels for 0%

profile of v1, /device:TPU:8, one launch (start us, length us, event | category | flops | bytes accessed | tf_op | source)
XLA Modules:
  0.0 847.7 jit_solution(11972497359706276061)
XLA Ops:
  8.2 1.9 collective-permute-start.8
  10.2 114.8 %all_gather.3 = bf16[1024,64]{1,0:T(8,128)(2,1)S(1)} all-gather(bf16[16,64]{1,0:T(8,128)(2,1)} %param.9), channel_id=1, replica_groups=mesh['ctx'=64,'ch'=8] {'ctx'}, dimensions={0}, use_global_device_ids=true | all-gather | bytes 133120 | tf_op jit(solution)/shard_map/all_gather | solution.py:55
  126.2 10.0 %all-to-all-start = ((bf16[8,1024,64]{1,2,0:T(8,128)(2,1)}), bf16[8,1024,64]{1,2,0:T(8,128)(2,1)S(1)}, u32[]{:S(2)}, u32[]{:S(2)}) async-start(bf16[8,1024,64]{1,2,0:T(8,128)(2,1)} %stack.71), calls=%async_computation | async-start | bytes 2097152 | tf_op jit(solution)/shard_map/all_to_all | solution.py:57
  136.4 1.9 collective-permute-start
  139.5 2.4 collective-permute-start.9
  141.9 35.8 %collective-permute-done = bf16[128,512]{1,0:T(8,128)(2,1)S(1)} collective-permute-done((bf16[128,512]{1,0:T(8,128)(2,1)S(1)}, bf16[128,512]{1,0:T(8,128)(2,1)S(1)}, u32[]{:S(2)}, u32[]{:S(2)}) %collective-permute-start) | collective-permute-done | bytes 131104 | tf_op jit(solution)/shard_map/ppermute | solution.py:13
  177.8 11.4 %collective-permute-start.1 = (bf16[128,512]{1,0:T(8,128)(2,1)S(1)}, bf16[128,512]{1,0:T(8,128)(2,1)S(1)}, u32[]{:S(2)}, u32[]{:S(2)}) collective-permute-start(bf16[128,512]{1,0:T(8,128)(2,1)S(1)} %collective-permute-done), channel_id=1, source_target_pairs={{8,0},{16,8},{24,16},{32,24},{40,32},{48,40},{56,48},{64,56},{72,6... | collective-permute-start | bytes 393224 | tf_op jit(solution)/shard_map/ppermute | solution.py:13
  189.2 1.9 collective-permute-start.10
  191.7 11.4 %collective-permute-start.2 = (bf16[128,512]{1,0:T(8,128)(2,1)S(1)}, bf16[128,512]{1,0:T(8,128)(2,1)S(1)}, u32[]{:S(2)}, u32[]{:S(2)}) collective-permute-start(bf16[128,512]{1,0:T(8,128)(2,1)S(1)} %collective-permute-done.1), channel_id=1, source_target_pairs={{8,0},{16,8},{24,16},{32,24},{40,32},{48,40},{56,48},{64,56},{72,6... | collective-permute-start | bytes 393224 | tf_op jit(solution)/shard_map/ppermute | solution.py:13
  203.1 1.9 collective-permute-start.11
  205.6 11.5 %collective-permute-start.3 = (bf16[128,512]{1,0:T(8,128)(2,1)S(1)}, bf16[128,512]{1,0:T(8,128)(2,1)S(1)}, u32[]{:S(2)}, u32[]{:S(2)}) collective-permute-start(bf16[128,512]{1,0:T(8,128)(2,1)S(1)} %collective-permute-done.2), channel_id=1, source_target_pairs={{8,0},{16,8},{24,16},{32,24},{40,32},{48,40},{56,48},{64,56},{72,6... | collective-permute-start | bytes 393224 | tf_op jit(solution)/shard_map/ppermute | solution.py:13
  217.2 1.9 collective-permute-start.12
  219.6 11.4 %collective-permute-start.4 = (bf16[128,512]{1,0:T(8,128)(2,1)S(1)}, bf16[128,512]{1,0:T(8,128)(2,1)S(1)}, u32[]{:S(2)}, u32[]{:S(2)}) collective-permute-start(bf16[128,512]{1,0:T(8,128)(2,1)S(1)} %collective-permute-done.3), channel_id=1, source_target_pairs={{8,0},{16,8},{24,16},{32,24},{40,32},{48,40},{56,48},{64,56},{72,6... | collective-permute-start | bytes 393224 | tf_op jit(solution)/shard_map/ppermute | solution.py:13
  231.1 1.9 collective-permute-start.13
  233.5 11.4 %collective-permute-start.5 = (bf16[128,512]{1,0:T(8,128)(2,1)S(1)}, bf16[128,512]{1,0:T(8,128)(2,1)S(1)}, u32[]{:S(2)}, u32[]{:S(2)}) collective-permute-start(bf16[128,512]{1,0:T(8,128)(2,1)S(1)} %collective-permute-done.4), channel_id=1, source_target_pairs={{8,0},{16,8},{24,16},{32,24},{40,32},{48,40},{56,48},{64,56},{72,6... | collective-permute-start | bytes 393224 | tf_op jit(solution)/shard_map/ppermute | solution.py:13
  244.9 1.9 collective-permute-start.14
  247.4 11.4 %collective-permute-start.6 = (bf16[128,512]{1,0:T(8,128)(2,1)S(1)}, bf16[128,512]{1,0:T(8,128)(2,1)S(1)}, u32[]{:S(2)}, u32[]{:S(2)}) collective-permute-start(bf16[128,512]{1,0:T(8,128)(2,1)S(1)} %collective-permute-done.5), channel_id=1, source_target_pairs={{8,0},{16,8},{24,16},{32,24},{40,32},{48,40},{56,48},{64,56},{72,6... | collective-permute-start | bytes 393224 | tf_op jit(solution)/shard_map/ppermute | solution.py:13
  258.8 1.9 collective-permute-start.15
  261.3 11.5 %collective-permute-start.7 = (bf16[128,512]{1,0:T(8,128)(2,1)S(1)}, bf16[128,512]{1,0:T(8,128)(2,1)S(1)}, u32[]{:S(2)}, u32[]{:S(2)}) collective-permute-start(bf16[128,512]{1,0:T(8,128)(2,1)S(1)} %collective-permute-done.6), channel_id=1, source_target_pairs={{8,0},{16,8},{24,16},{32,24},{40,32},{48,40},{56,48},{64,56},{72,6... | collective-permute-start | bytes 393224 | tf_op jit(solution)/shard_map/ppermute | solution.py:13
  272.8 2.3 collective-permute-done.7
  275.1 2.3 convolution_bitcast_fusion.1
  277.5 2.4 convolution_bitcast_fusion
  280.8 1.6 copy-done
  283.3 7.3 fusion.7
  291.6 3.8 convolution_bitcast_fusion.2
  295.5 3.6 subtract_reduce_fusion
  300.5 1.4 fusion.25
  301.9 392.9 %reduce-scatter.5.cloned.1.call-done = f32[16,512]{1,0:T(8,128)} async-done(((f32[1024,512]{1,0:T(8,128)}), f32[16,512]{1,0:T(8,128)}) %reduce-scatter.5.cloned.1.call-update) | async-done | bytes 32784 | tf_op jit(solution)/shard_map/reduce_scatter | solution.py:118
  694.8 1.6 copy.13
  696.4 1.3 fusion.11
  697.7 141.8 %reduce-scatter.7.cloned.1.call-done = f32[64,16]{1,0:T(8,128)} async-done(((f32[512,16]{1,0:T(8,128)}), f32[64,16]{1,0:T(8,128)}) %reduce-scatter.7.cloned.1.call-update) | async-done | bytes 4112
  839.5 1.4 copy.14
  (72 shorter events, 11.1 us)
Async XLA Ops:
  7.2 129.2 %copy-start.5 = (bf16[128,512]{1,0:T(8,128)(2,1)S(1)}, bf16[128,512]{1,0:T(8,128)(2,1)}, u32[]{:S(2)}) copy-start(bf16[128,512]{1,0:T(8,128)(2,1)} %param.6) | copy-start | bytes 393220
  7.2 129.2 %copy-start.4 = (bf16[128,512]{1,0:T(8,128)(2,1)S(1)}, bf16[128,512]{1,0:T(8,128)(2,1)}, u32[]{:S(2)}) copy-start(bf16[128,512]{1,0:T(8,128)(2,1)} %param.8) | copy-start | bytes 393220
  8.2 131.3 %collective-permute-start.8 = (bf16[128,512]{1,0:T(8,128)(2,1)S(1)}, bf16[128,512]{1,0:T(8,128)(2,1)S(1)}, u32[]{:S(2)}, u32[]{:S(2)}) collective-permute-start(bf16[128,512]{1,0:T(8,128)(2,1)S(1)} %get-tuple-element.13), channel_id=1, source_target_pairs={{0,8},{8,16},{16,24},{24,32},{32,40},{40,48},{48,56},{56,64},{64,7... | collective-permute-start | bytes 393224 | tf_op jit(solution)/shard_map/ppermute | solution.py:13
  126.2 164.6 %all-to-all-start = ((bf16[8,1024,64]{1,2,0:T(8,128)(2,1)}), bf16[8,1024,64]{1,2,0:T(8,128)(2,1)S(1)}, u32[]{:S(2)}, u32[]{:S(2)}) async-start(bf16[8,1024,64]{1,2,0:T(8,128)(2,1)} %stack.71), calls=%async_computation | async-start | bytes 2097152 | tf_op jit(solution)/shard_map/all_to_all | solution.py:57
  136.3 558.5 %reduce-scatter.5.cloned.1.call-start = ((), (), s32[]{:S(2)}) async-start(), calls=%async_computation.3 | async-start | bytes 2129920 | tf_op jit(solution)/shard_map/reduce_scatter | solution.py:118
  136.4 41.4 %collective-permute-start = (bf16[128,512]{1,0:T(8,128)(2,1)S(1)}, bf16[128,512]{1,0:T(8,128)(2,1)S(1)}, u32[]{:S(2)}, u32[]{:S(2)}) collective-permute-start(bf16[128,512]{1,0:T(8,128)(2,1)S(1)} %get-tuple-element.15), channel_id=1, source_target_pairs={{8,0},{16,8},{24,16},{32,24},{40,32},{48,40},{56,48},{64,56},{72,6... | collective-permute-start | bytes 393224 | tf_op jit(solution)/shard_map/ppermute | solution.py:13
  139.5 49.7 %collective-permute-start.9 = (bf16[128,512]{1,0:T(8,128)(2,1)S(1)}, bf16[128,512]{1,0:T(8,128)(2,1)S(1)}, u32[]{:S(2)}, u32[]{:S(2)}) collective-permute-start(bf16[128,512]{1,0:T(8,128)(2,1)S(1)} %collective-permute-done.8), channel_id=1, source_target_pairs={{0,8},{8,16},{16,24},{24,32},{32,40},{40,48},{48,56},{56,64},{64,7... | collective-permute-start | bytes 393224 | tf_op jit(solution)/shard_map/ppermute | solution.py:13
  177.8 13.9 %collective-permute-start.1 = (bf16[128,512]{1,0:T(8,128)(2,1)S(1)}, bf16[128,512]{1,0:T(8,128)(2,1)S(1)}, u32[]{:S(2)}, u32[]{:S(2)}) collective-permute-start(bf16[128,512]{1,0:T(8,128)(2,1)S(1)} %collective-permute-done), channel_id=1, source_target_pairs={{8,0},{16,8},{24,16},{32,24},{40,32},{48,40},{56,48},{64,56},{72,6... | collective-permute-start | bytes 393224 | tf_op jit(solution)/shard_map/ppermute | solution.py:13
  189.2 13.9 %collective-permute-start.10 = (bf16[128,512]{1,0:T(8,128)(2,1)S(1)}, bf16[128,512]{1,0:T(8,128)(2,1)S(1)}, u32[]{:S(2)}, u32[]{:S(2)}) collective-permute-start(bf16[128,512]{1,0:T(8,128)(2,1)S(1)} %collective-permute-done.9), channel_id=1, source_target_pairs={{0,8},{8,16},{16,24},{24,32},{32,40},{40,48},{48,56},{56,64},{64,7... | collective-permute-start | bytes 393224 | tf_op jit(solution)/shard_map/ppermute | solution.py:13
  191.7 13.9 %collective-permute-start.2 = (bf16[128,512]{1,0:T(8,128)(2,1)S(1)}, bf16[128,512]{1,0:T(8,128)(2,1)S(1)}, u32[]{:S(2)}, u32[]{:S(2)}) collective-permute-start(bf16[128,512]{1,0:T(8,128)(2,1)S(1)} %collective-permute-done.1), channel_id=1, source_target_pairs={{8,0},{16,8},{24,16},{32,24},{40,32},{48,40},{56,48},{64,56},{72,6... | collective-permute-start | bytes 393224 | tf_op jit(solution)/shard_map/ppermute | solution.py:13
  203.1 14.0 %collective-permute-start.11 = (bf16[128,512]{1,0:T(8,128)(2,1)S(1)}, bf16[128,512]{1,0:T(8,128)(2,1)S(1)}, u32[]{:S(2)}, u32[]{:S(2)}) collective-permute-start(bf16[128,512]{1,0:T(8,128)(2,1)S(1)} %collective-permute-done.10), channel_id=1, source_target_pairs={{0,8},{8,16},{16,24},{24,32},{32,40},{40,48},{48,56},{56,64},{64,7... | collective-permute-start | bytes 393224 | tf_op jit(solution)/shard_map/ppermute | solution.py:13
  205.6 14.0 %collective-permute-start.3 = (bf16[128,512]{1,0:T(8,128)(2,1)S(1)}, bf16[128,512]{1,0:T(8,128)(2,1)S(1)}, u32[]{:S(2)}, u32[]{:S(2)}) collective-permute-start(bf16[128,512]{1,0:T(8,128)(2,1)S(1)} %collective-permute-done.2), channel_id=1, source_target_pairs={{8,0},{16,8},{24,16},{32,24},{40,32},{48,40},{56,48},{64,56},{72,6... | collective-permute-start | bytes 393224 | tf_op jit(solution)/shard_map/ppermute | solution.py:13
  217.2 14.0 %collective-permute-start.12 = (bf16[128,512]{1,0:T(8,128)(2,1)S(1)}, bf16[128,512]{1,0:T(8,128)(2,1)S(1)}, u32[]{:S(2)}, u32[]{:S(2)}) collective-permute-start(bf16[128,512]{1,0:T(8,128)(2,1)S(1)} %collective-permute-done.11), channel_id=1, source_target_pairs={{0,8},{8,16},{16,24},{24,32},{32,40},{40,48},{48,56},{56,64},{64,7... | collective-permute-start | bytes 393224 | tf_op jit(solution)/shard_map/ppermute | solution.py:13
  219.6 13.9 %collective-permute-start.4 = (bf16[128,512]{1,0:T(8,128)(2,1)S(1)}, bf16[128,512]{1,0:T(8,128)(2,1)S(1)}, u32[]{:S(2)}, u32[]{:S(2)}) collective-permute-start(bf16[128,512]{1,0:T(8,128)(2,1)S(1)} %collective-permute-done.3), channel_id=1, source_target_pairs={{8,0},{16,8},{24,16},{32,24},{40,32},{48,40},{56,48},{64,56},{72,6... | collective-permute-start | bytes 393224 | tf_op jit(solution)/shard_map/ppermute | solution.py:13
  231.1 13.8 %collective-permute-start.13 = (bf16[128,512]{1,0:T(8,128)(2,1)S(1)}, bf16[128,512]{1,0:T(8,128)(2,1)S(1)}, u32[]{:S(2)}, u32[]{:S(2)}) collective-permute-start(bf16[128,512]{1,0:T(8,128)(2,1)S(1)} %collective-permute-done.12), channel_id=1, source_target_pairs={{0,8},{8,16},{16,24},{24,32},{32,40},{40,48},{48,56},{56,64},{64,7... | collective-permute-start | bytes 393224 | tf_op jit(solution)/shard_map/ppermute | solution.py:13
  233.5 13.9 %collective-permute-start.5 = (bf16[128,512]{1,0:T(8,128)(2,1)S(1)}, bf16[128,512]{1,0:T(8,128)(2,1)S(1)}, u32[]{:S(2)}, u32[]{:S(2)}) collective-permute-start(bf16[128,512]{1,0:T(8,128)(2,1)S(1)} %collective-permute-done.4), channel_id=1, source_target_pairs={{8,0},{16,8},{24,16},{32,24},{40,32},{48,40},{56,48},{64,56},{72,6... | collective-permute-start | bytes 393224 | tf_op jit(solution)/shard_map/ppermute | solution.py:13
  244.9 13.9 %collective-permute-start.14 = (bf16[128,512]{1,0:T(8,128)(2,1)S(1)}, bf16[128,512]{1,0:T(8,128)(2,1)S(1)}, u32[]{:S(2)}, u32[]{:S(2)}) collective-permute-start(bf16[128,512]{1,0:T(8,128)(2,1)S(1)} %collective-permute-done.13), channel_id=1, source_target_pairs={{0,8},{8,16},{16,24},{24,32},{32,40},{40,48},{48,56},{56,64},{64,7... | collective-permute-start | bytes 393224 | tf_op jit(solution)/shard_map/ppermute | solution.py:13
  247.4 13.9 %collective-permute-start.6 = (bf16[128,512]{1,0:T(8,128)(2,1)S(1)}, bf16[128,512]{1,0:T(8,128)(2,1)S(1)}, u32[]{:S(2)}, u32[]{:S(2)}) collective-permute-start(bf16[128,512]{1,0:T(8,128)(2,1)S(1)} %collective-permute-done.5), channel_id=1, source_target_pairs={{8,0},{16,8},{24,16},{32,24},{40,32},{48,40},{56,48},{64,56},{72,6... | collective-permute-start | bytes 393224 | tf_op jit(solution)/shard_map/ppermute | solution.py:13
  258.8 18.7 %collective-permute-start.15 = (bf16[128,512]{1,0:T(8,128)(2,1)S(1)}, bf16[128,512]{1,0:T(8,128)(2,1)S(1)}, u32[]{:S(2)}, u32[]{:S(2)}) collective-permute-start(bf16[128,512]{1,0:T(8,128)(2,1)S(1)} %collective-permute-done.14), channel_id=1, source_target_pairs={{0,8},{8,16},{16,24},{24,32},{32,40},{40,48},{48,56},{56,64},{64,7... | collective-permute-start | bytes 393224 | tf_op jit(solution)/shard_map/ppermute | solution.py:13
  261.3 13.8 %collective-permute-start.7 = (bf16[128,512]{1,0:T(8,128)(2,1)S(1)}, bf16[128,512]{1,0:T(8,128)(2,1)S(1)}, u32[]{:S(2)}, u32[]{:S(2)}) collective-permute-start(bf16[128,512]{1,0:T(8,128)(2,1)S(1)} %collective-permute-done.6), channel_id=1, source_target_pairs={{8,0},{16,8},{24,16},{32,24},{40,32},{48,40},{56,48},{64,56},{72,6... | collective-permute-start | bytes 393224 | tf_op jit(solution)/shard_map/ppermute | solution.py:13
  277.4 2.5 copy-start.1
  279.9 2.5 copy-start
  290.5 548.9 %reduce-scatter.7.cloned.1.call-start = ((), (), s32[]{:S(2)}) async-start(), calls=%async_computation.4 | async-start | bytes 294912
  290.8 4.6 slice-start
  290.8 4.6 slice-start.2
  291.1 4.3 slice-start.1
  291.1 4.3 slice-start.3
  295.5 5.0 copy-start.2
  295.5 5.0 copy-start.3
Sparse Core Ops, SparseCore 0:
  290.7 404.0 reduce-scatter.4
  699.8 139.5 reduce-scatter.6
